TPU v7x, 32 devices: a whole 2x2x4 slice. The times are simulated.
32 devices in a mesh: row: 8 (over z, x), col: 4 (over y, core).
Axes of the slice: x: 2, y: 2, z: 4, core: 2. Of those that a mesh axis runs over, the one named last changes fastest.
Arguments:
- tokens: bfloat16 [4, 320, 768], P(None, 'row'), may hold values from -6 to 6
- single_cond: bfloat16 [320, 384], P('row'), may hold values from -6 to 6
- pair_cond: float32 [320, 320, 128], P('row', 'col'), may hold values from -8 to 8
- ada_gain: float32 [2, 384], replicated, may hold values from 0.1 to 1.9
- ada_scale_w: bfloat16 [2, 384, 768], P(None, None, 'col'), may hold values from -0.3125 to 0.3125
- ada_scale_b: float32 [2, 768], P(None, 'col'), may hold values from -4 to 4
- adaptive_shift_weight: bfloat16 [2, 384, 768], P(None, None, 'col'), may hold values from -0.3125 to 0.3125
- pair_gain: float32 [128], replicated, may hold values from 0.1 to 1.9
- pair_proj: float32 [128, 16], replicated, may hold values from -8 to 8
- qkvg_weight: bfloat16 [4, 768, 768], P(None, None, 'col'), may hold values from -0.21875 to 0.21875
- query_bias: float32 [768], P('col'), may hold values from -4 to 4
- output_weight: bfloat16 [768, 768], P('col'), may hold values from -0.21875 to 0.21875
- out_gate_w: bfloat16 [2, 384, 768], P(None, None, 'col'), may hold values from -0.3125 to 0.3125
- out_gate_b: float32 [2, 768], P(None, 'col'), may hold values from -4 to 4
- transition_input_weight: bfloat16 [2, 768, 1536], P(None, None, 'col'), may hold values from -0.21875 to 0.21875
- trans_out: bfloat16 [1536, 768], P('col'), may hold values from -0.15625 to 0.15625
Outputs:
- mixed: bfloat16 [4, 320, 768], P(None, 'row', 'col')
All inputs are finite; a program needn't handle non-finite values.
Results may differ from a plain program's by a relative error of at most 0.0052.
Values may be sent and summed in bfloat16 or wider, within the bound.
A program may use at most 64 MiB of HBM per device.

v0:
```python
import math

import jax
import jax.numpy as jnp
from jax import lax
from jax.sharding import PartitionSpec as P

D = 768
H = 16


epsilon = 1e-05


def layer_norm(values):
    center = values - jnp.mean(values, axis=-1, keepdims=True)
    spread = jnp.mean(center * center, axis=-1, keepdims=True)
    return center * lax.rsqrt(spread + epsilon)


def shards(
    tokens,
    single_cond,
    pair_cond,
    ada_gain,
    ada_scale_w,
    ada_scale_b,
    adaptive_shift_weight,
    pair_gain,
    pair_proj,
    qkvg_weight,
    query_bias,
    output_weight,
    out_gate_w,
    out_gate_b,
    transition_input_weight,
    trans_out,
):
    samples, local_rows, full_width = tokens.shape
    width_shard = qkvg_weight.shape[2]
    head_size = D // H
    heads_here = width_shard // head_size
    cond = (layer_norm(single_cond.astype(jnp.float32))[None] * ada_gain[:, None, :]).astype(
        jnp.bfloat16
    )

    def scale_of(index):
        return jax.nn.sigmoid(
            jnp.dot(cond[index], ada_scale_w[index], preferred_element_type=jnp.float32)
            + ada_scale_b[index]
        )

    def shift_of(index):
        return jnp.dot(
            cond[index], adaptive_shift_weight[index], preferred_element_type=jnp.float32
        )

    def gate_of(index):
        return jax.nn.sigmoid(
            jnp.dot(cond[index], out_gate_w[index], preferred_element_type=jnp.float32)
            + out_gate_b[index]
        )

    stacked = jnp.stack([scale_of(0), shift_of(0), gate_of(0), scale_of(1), shift_of(1)])
    mods = lax.all_gather(stacked, "col", axis=2, tiled=True)
    final_gate = gate_of(1)
    pair_normed = layer_norm(pair_cond) * pair_gain
    bias = jnp.einsum("ijc,ch->hij", pair_normed, pair_proj, precision=lax.Precision.HIGHEST)
    bias_rows = lax.all_to_all(bias, "col", split_axis=0, concat_axis=2, tiled=True)
    stream = tokens.astype(jnp.float32)
    norm_in = (mods[0] * layer_norm(stream) + mods[1]).astype(jnp.bfloat16)
    project = jnp.einsum("std,edf->estf", norm_in, qkvg_weight, preferred_element_type=jnp.float32)
    query = (project[0] + query_bias).astype(jnp.bfloat16)
    key_rows = project[1].astype(jnp.bfloat16)
    value_rows = project[2].astype(jnp.bfloat16)
    gates = jax.nn.sigmoid(project[3])
    query_heads = query.reshape(samples, local_rows, heads_here, head_size)
    best = jnp.full((samples, heads_here, local_rows), -1e30, jnp.float32)
    key_piece = lax.all_gather(key_rows, "row", axis=1, tiled=True)
    value_piece = lax.all_gather(value_rows, "row", axis=1, tiled=True)
    count = key_piece.shape[1]
    key_heads = key_piece.reshape(samples, count, heads_here, head_size)
    value_heads = value_piece.reshape(samples, count, heads_here, head_size).astype(jnp.float32)
    scores = (
        jnp.einsum("sqhd,skhd->shqk", query_heads, key_heads, preferred_element_type=jnp.float32)
        / math.sqrt(head_size)
        + bias_rows[None]
    )
    peak = jnp.maximum(best, jnp.max(scores, axis=-1))
    weight = jnp.exp(scores - peak[..., None])
    total = jnp.sum(weight, axis=-1)
    accum = jnp.einsum("shqk,skhd->shqd", weight, value_heads, precision=lax.Precision.HIGHEST)
    best, total, accum = (peak, total, accum)
    heads_out = jnp.transpose(accum / total[..., None], (0, 2, 1, 3)).reshape(
        samples, local_rows, width_shard
    )
    attention_result = (gates * heads_out).astype(jnp.bfloat16)
    partial_terms = jnp.einsum(
        "stl,ld->std", attention_result, output_weight, preferred_element_type=jnp.float32
    )
    projected_output = lax.psum(partial_terms, "col")
    resid = stream + mods[2] * projected_output
    middle_norm = (mods[3] * layer_norm(resid) + mods[4]).astype(jnp.bfloat16)
    inner = jnp.einsum(
        "std,edf->estf", middle_norm, transition_input_weight, preferred_element_type=jnp.float32
    )
    hidden = (jax.nn.silu(inner[0]) * inner[1]).astype(jnp.bfloat16)
    terms = jnp.einsum("stl,ld->std", hidden, trans_out, preferred_element_type=jnp.float32)
    outward = lax.psum_scatter(terms, "col", scatter_dimension=2, tiled=True)
    out_width = final_gate.shape[1]
    column = lax.axis_index("col") * out_width
    resid_here = lax.dynamic_slice_in_dim(resid, column, out_width, 2)
    mixed = resid_here + final_gate * outward
    return mixed.astype(jnp.bfloat16)


def solution(mesh):
    return jax.shard_map(
        shards,
        mesh=mesh,
        in_specs=(
            P(None, "row", None),
            P("row", None),
            P("row", "col", None),
            P(),
            P(None, None, "col"),
            P(None, "col"),
            P(None, None, "col"),
            P(),
            P(),
            P(None, None, "col"),
            P("col"),
            P("col", None),
            P(None, None, "col"),
            P(None, "col"),
            P(None, None, "col"),
            P("col", None),
        ),
        out_specs=P(None, "row", "col"),
        check_vma=False,
    )
```

profile of v0, /device:TPU:9, one launch (start us, length us, event | category | flops | bytes accessed | tf_op | source)
XLA Modules:
  0.0 194.2 jit_solution(17073160385300619404)
XLA Ops:
  6.5 2.3 %reduce_sum.85 = f32[40,80]{1,0:T(8,128)S(1)} reduce(f32[40,80,128]{2,1,0:T(8,128)} %param.18, f32[]{:T(128)} %constant.14.clone.1), dimensions={2}, to_apply=%region_4.0 | reduce | flops 406400 | bytes 1651204 | tf_op jit(solution)/shard_map/reduce_sum | solution.py:16
  8.9 1.2 multiply_reduce_fusion
  10.2 4.3 %fusion.5 = f32[16,40,80]{2,0,1:T(8,128)S(1)} fusion(f32[40,80,128]{2,1,0:T(8,128)S(1)} %copy-done.1, f32[128]{0:T(128)S(1)} %copy-done.16, f32[40,80]{1,0:T(8,128)S(1)} %add_rsqrt_fusion, f32[40,80]{1,0:T(8,128)S(1)} %broadcast_multiply_fusion, f32[128,16]{0,1:T(8,128)S(1)} %copy-done.11), kind=kOutput, calls=%fused_computation.9 | convolution fusion | flops 79872000 | bytes 1877504 | tf_op jit(solution)/shard_map/ijc,ch->hij/dot_general | solution.py:68
  14.6 0.8 copy.35
  15.4 4.7 %all-to-all-start = ((f32[16,40,80]{2,1,0:T(8,128)}), f32[16,40,80]{2,1,0:T(8,128)}, u32[]{:S(2)}, u32[]{:S(2)}) async-start(f32[16,40,80]{2,1,0:T(8,128)} %copy.35), calls=%async_computation | async-start | bytes 655360 | tf_op jit(solution)/shard_map/all_to_all | solution.py:69
  20.2 0.2 fusion.91
  20.6 0.2 fusion.34
  20.8 0.2 fusion.28
  21.0 0.2 fusion.27
  21.2 0.2 fusion.21
  21.4 0.2 fusion.15
  21.6 0.3 copy.29
  22.0 22.7 %all_gather.9 = f32[5,40,768]{1,0,2:T(8,128)S(1)} all-gather(f32[5,40,192]{1,0,2:T(8,128)S(1)} %copy.29), channel_id=1, replica_groups=mesh['row'=8,'col'=4] {'col'}, dimensions={2}, use_global_device_ids=true | all-gather | bytes 768000 | tf_op jit(solution)/shard_map/all_gather | solution.py:65
  44.7 2.1 %fusion.96 = (f32[1,40,768]{1,0,2:T(1,128)S(1)}, f32[1,40,768]{1,0,2:T(1,128)S(1)}, f32[1,40,768]{1,0,2:T(1,128)S(1)}, f32[1,40,768]{1,0,2:T(1,128)S(1)}, f32[1,40,768]{1,0,2:T(1,128)}) fusion(f32[5,40,768]{1,0,2:T(8,128)S(1)} %all_gather.9), kind=kLoop, calls=%fused_computation.125 | loop fusion | bytes 1228800 | tf_op jit(solution)/shard_map/slice | solution.py:103
  46.8 0.1 copy.31
  46.9 0.1 copy.32
  47.2 0.2 fusion.43
  47.5 1.5 fusion.100
  48.9 23.4 %all-gather = bf16[1,4,320,192]{3,2,0,1:T(8,128)(2,1)S(1)} all-gather(bf16[1,4,40,192]{3,2,0,1:T(8,128)(2,1)S(1)} %get-tuple-element.12), channel_id=2, replica_groups=mesh['row'=8,'col'=4] {'row'}, dimensions={2}, use_global_device_ids=true | all-gather | bytes 552960 | tf_op jit(solution)/shard_map/all_gather | solution.py:79
  72.4 0.3 copy.34
  72.7 0.9 slice.104
  73.6 0.9 squeeze.47
  74.7 25.7 %all-gather.1 = bf16[1,4,320,192]{3,2,0,1:T(8,128)(2,1)S(1)} all-gather(bf16[1,4,40,192]{3,2,0,1:T(8,128)(2,1)S(1)} %get-tuple-element.13), channel_id=3, replica_groups=mesh['row'=8,'col'=4] {'row'}, dimensions={2}, use_global_device_ids=true | all-gather | bytes 552960 | tf_op jit(solution)/shard_map/all_gather | solution.py:80
  100.4 1.1 copy.37
  101.5 1.2 copy.36
  102.7 0.2 add.176
  102.9 1.4 fusion.101
  104.3 0.4 fusion.35
  104.7 0.9 fusion.8
  105.7 0.2 reshape.82
  105.9 1.9 %fusion.49 = f32[4,40,768]{2,1,0:T(8,128)} fusion(bf16[192,768]{1,0:T(8,128)(2,1)S(1)} %copy-done.7, f32[4,40,192]{2,1,0:T(8,128)S(1)} %reshape.82, f32[4,4,40,192]{3,2,0,1:T(8,128)} %get-tuple-element.19), kind=kOutput, calls=%fused_computation.65 | convolution fusion | flops 47339520 | bytes 1073152 | tf_op jit(solution)/shard_map/stl,ld->std/dot_general | solution.py:98
  107.8 0.2 reduce-scatter.4.cloned.1.call-start
  108.1 0.8 copy.30
  108.9 0.1 copy.39
  109.0 0.1 copy.40
  109.2 45.0 %all-reduce.2.cloned.1.call-done = f32[4,40,768]{2,1,0:T(8,128)} async-done(((f32[4,40,768]{2,1,0:T(8,128)}), f32[4,40,768]{2,1,0:T(8,128)}) %all-reduce.2.cloned.1.call-update) | async-done | bytes 491536 | tf_op jit(solution)/shard_map/psum | solution.py:101
  154.2 1.2 fusion.95
  155.4 0.2 multiply_reduce_fusion.1
  155.6 0.5 convolution_bitcast_fusion.1
  156.1 0.4 copy-done.17
  156.5 1.1 fusion.39
  157.6 1.6 copy.44
  159.2 1.6 reshape.94
  160.8 1.1 fusion.14
  161.9 23.3 %reduce-scatter.4.cloned.1.call-done = f32[192,160]{1,0:T(8,128)} async-done(((f32[768,160]{1,0:T(8,128)}), f32[192,160]{1,0:T(8,128)}) %reduce-scatter.4.cloned.1.call-update) | async-done | bytes 122896
  185.2 1.1 reshape.95
  186.4 0.2 copy.45
  186.6 0.8 add_convert_fusion.1
  (61 shorter events, 0.7 us)
Async XLA Ops:
  6.5 40.9 %copy-start = (bf16[4,768,192]{1,2,0:T(8,128)(2,1)S(1)}, bf16[4,768,192]{1,2,0:T(8,128)(2,1)}, u32[]{:S(2)}) copy-start(bf16[4,768,192]{1,2,0:T(8,128)(2,1)} %param.25) | copy-start | bytes 3538948
  6.5 2.3 %copy-start.1 = (f32[40,80,128]{2,1,0:T(8,128)S(1)}, f32[40,80,128]{2,1,0:T(8,128)}, u32[]{:S(2)}) copy-start(f32[40,80,128]{2,1,0:T(8,128)} %param.18) | copy-start | bytes 4915204
  6.5 3.6 %copy-start.16 = (f32[128]{0:T(128)S(1)}, f32[128]{0:T(128)}, u32[]{:S(2)}) copy-start(f32[128]{0:T(128)} %param.23) | copy-start | bytes 1540
  6.5 3.6 %copy-start.11 = (f32[128,16]{0,1:T(8,128)S(1)}, f32[128,16]{0,1:T(8,128)}, u32[]{:S(2)}) copy-start(f32[128,16]{0,1:T(8,128)} %param.24) | copy-start | bytes 24580
  10.1 10.0 %copy-start.8 = (bf16[40,384]{1,0:T(8,128)(2,1)S(1)}, bf16[40,384]{1,0:T(8,128)(2,1)}, u32[]{:S(2)}) copy-start(bf16[40,384]{1,0:T(8,128)(2,1)} %param.17) | copy-start | bytes 92164
  10.1 10.4 %copy-start.13 = (f32[2,192]{1,0:T(2,128)S(1)}, f32[2,192]{1,0:T(2,128)}, u32[]{:S(2)}) copy-start(f32[2,192]{1,0:T(2,128)} %param.21) | copy-start | bytes 4612
  10.2 10.4 %copy-start.14 = (f32[2,192]{1,0:T(2,128)S(1)}, f32[2,192]{1,0:T(2,128)}, u32[]{:S(2)}) copy-start(f32[2,192]{1,0:T(2,128)} %param.29) | copy-start | bytes 4612
  10.2 10.4 %copy-start.12 = (f32[2,384]{1,0:T(2,128)S(1)}, f32[2,384]{1,0:T(2,128)}, u32[]{:S(2)}) copy-start(f32[2,384]{1,0:T(2,128)} %param.19) | copy-start | bytes 9220
  10.2 10.5 %copy-start.18 = (bf16[2,384,192]{1,2,0:T(8,128)(2,1)S(1)}, bf16[2,384,192]{1,2,0:T(8,128)(2,1)}, u32[]{:S(2)}) copy-start(bf16[2,384,192]{1,2,0:T(8,128)(2,1)} %param.20) | copy-start | bytes 884740
  10.2 10.6 %copy-start.6 = (bf16[2,384,192]{1,2,0:T(8,128)(2,1)S(1)}, bf16[2,384,192]{1,2,0:T(8,128)(2,1)}, u32[]{:S(2)}) copy-start(bf16[2,384,192]{1,2,0:T(8,128)(2,1)} %param.22) | copy-start | bytes 884740
  14.5 6.5 %copy-start.19 = (bf16[2,384,192]{1,2,0:T(8,128)(2,1)S(1)}, bf16[2,384,192]{1,2,0:T(8,128)(2,1)}, u32[]{:S(2)}) copy-start(bf16[2,384,192]{1,2,0:T(8,128)(2,1)} %param.28) | copy-start | bytes 884740
  15.4 86.1 %all-to-all-start = ((f32[16,40,80]{2,1,0:T(8,128)}), f32[16,40,80]{2,1,0:T(8,128)}, u32[]{:S(2)}, u32[]{:S(2)}) async-start(f32[16,40,80]{2,1,0:T(8,128)} %copy.35), calls=%async_computation | async-start | bytes 655360 | tf_op jit(solution)/shard_map/all_to_all | solution.py:69
  20.1 134.1 %all-reduce.2.cloned.1.call-start = ((), (), s32[]{:S(2)}) async-start(), calls=%async_computation.2 | async-start | bytes 983040 | tf_op jit(solution)/shard_map/psum | solution.py:101
  20.6 0.8 copy-start.9
  44.7 2.4 %copy-start.2 = (bf16[4,40,768]{2,1,0:T(8,128)(2,1)S(1)}, bf16[4,40,768]{2,1,0:T(8,128)(2,1)}, u32[]{:S(2)}) copy-start(bf16[4,40,768]{2,1,0:T(8,128)(2,1)} %param.16) | copy-start | bytes 737284
  48.9 25.6 %copy-start.15 = (f32[192]{0:T(256)S(1)}, f32[192]{0:T(256)}, u32[]{:S(2)}) copy-start(f32[192]{0:T(256)} %param.26) | copy-start | bytes 2308
  102.8 1.8 copy-start.5
  104.7 1.2 copy-start.7
  105.6 2.5 %copy-start.3 = (f32[1,40,768]{1,0,2:T(1,128)S(1)}, f32[1,40,768]{1,0,2:T(1,128)}, u32[]{:S(2)}) copy-start(f32[1,40,768]{1,0,2:T(1,128)} %get-tuple-element.11) | copy-start | bytes 368644
  107.8 77.4 %reduce-scatter.4.cloned.1.call-start = ((), (), s32[]{:S(2)}) async-start(), calls=%async_computation.3 | async-start | bytes 983040
  108.9 46.8 %copy-start.4 = (bf16[2,768,384]{2,1,0:T(8,128)(2,1)S(1)}, bf16[2,768,384]{2,1,0:T(8,128)(2,1)}, u32[]{:S(2)}) copy-start(bf16[2,768,384]{2,1,0:T(8,128)(2,1)} %param.30) | copy-start | bytes 3538948
  155.4 1.1 copy-start.17
  159.2 1.6 copy-start.10
Sparse Core Ops, SparseCore 0:
  108.0 46.2 all-reduce.1
  160.9 24.2 reduce-scatter.3
where the time goes:
time: 196 us; the launch traced here: 194 us
  blocking collectives  71.8 us (37%)
  waiting for transfers between devices  68.4 us (35%)
  local copies, waits for them, and re-layouts  14.7 us (8%)
  between operations  13.9 us (7%)
  matrix products  13.6 us (7%)
  other arithmetic  6.79 us (3%)
  starting transfers between devices  4.95 us (3%)
    psum x1, waiting for transfers between devices, shards(): projected_output = lax.psum(partial_terms, 'col')  45 us
    all_gather x1, blocking collectives, shards(): value_piece = lax.all_gather(value_rows, 'row', axis=1, tiled=True)  25.7 us
    all_gather x1, blocking collectives, shards(): key_piece = lax.all_gather(key_rows, 'row', axis=1, tiled=True)  23.4 us
    unnamed x3, waiting for transfers between devices  23.4 us
    all_gather x1, blocking collectives, shards(): mods = lax.all_gather(stacked, 'col', axis=2, tiled=True)  22.7 us
    unnamed x44, local copies, waits for them, and re-layouts  4.96 us
    all_to_all x1, starting transfers between devices, shards(): lax.all_to_all(bias, 'col', split_axis=0, concat_axis=2, tiled=True)  4.73 us
    dot_general x1, matrix products, shards(): jnp.einsum('ijc,ch->hij', pair_normed, pair_proj, precision=lax.Precision...  4.34 us
  transfers between devices with their start and end apart: 3, of which 2 were waited for; matrix products, arithmetic and copies ran while one was open for 6% of the time, Pallas kernels for 0%

commit v1 on v0

v1 whole, which is shorter than its diff:
```python
import functools
import math

import jax
import jax.numpy as jnp
from jax import lax
from jax.experimental import pallas as pl
from jax.experimental.pallas import tpu as pltpu
from jax.sharding import PartitionSpec as P

H = 16
epsilon = 1e-05
F32 = jnp.float32
BF16 = jnp.bfloat16


def layer_norm(values):
    center = values - jnp.mean(values, axis=-1, keepdims=True)
    spread = jnp.mean(center * center, axis=-1, keepdims=True)
    return center * lax.rsqrt(spread + epsilon)


def dot(a, b):
    return jnp.dot(a, b, preferred_element_type=F32)


def dot_t(a, b):
    return lax.dot_general(a, b, (((1,), (1,)), ((), ())), preferred_element_type=F32)


class Exchange:
    def __init__(self, axis, n, source, buffer, send, recv):
        self.axis, self.n, self.source, self.buffer = axis, n, source, buffer
        self.send, self.recv = send, recv
        self.me = lax.axis_index(axis)

    def copy(self, d):
        target = lax.rem(self.me + d, self.n)
        return pltpu.make_async_remote_copy(
            src_ref=self.source(target),
            dst_ref=self.buffer.at[self.me],
            send_sem=self.send.at[d],
            recv_sem=self.recv.at[self.me],
            device_id={self.axis: target},
            device_id_type=pl.DeviceIdType.MESH,
        )

    def start(self):
        for d in range(1, self.n):
            self.copy(d).start()

    def arrive(self):
        for d in range(1, self.n):
            origin = lax.rem(self.me + d, self.n)
            pltpu.make_async_remote_copy(
                src_ref=self.buffer.at[origin],
                dst_ref=self.buffer.at[origin],
                send_sem=self.send.at[d],
                recv_sem=self.recv.at[origin],
                device_id={self.axis: origin},
                device_id_type=pl.DeviceIdType.MESH,
            ).wait_recv()

    def drain(self):
        for d in range(1, self.n):
            self.copy(d).wait_send()


class PairGather:
    def __init__(self, axis, n, buffer, send, handed, recv):
        self.axis, self.n, self.buffer = axis, n, buffer
        self.send, self.handed, self.recv = send, handed, recv
        self.me = lax.axis_index(axis)
        self.partner = self.me + 1 - 2 * lax.rem(self.me, 2)

    def copy(self, block, target, sem):
        return pltpu.make_async_remote_copy(
            src_ref=self.buffer.at[block],
            dst_ref=self.buffer.at[block],
            send_sem=sem,
            recv_sem=self.recv.at[block],
            device_id={self.axis: target},
            device_id_type=pl.DeviceIdType.MESH,
        )

    def mate(self, d):
        return lax.rem(self.me + 2 * d, self.n)

    def start(self):
        for d in range(1, self.n // 2):
            self.copy(self.me, self.mate(d), self.send.at[d]).start()
        self.copy(self.me, self.partner, self.send.at[0]).start()

    def hand_on(self):
        for d in range(1, self.n // 2):
            block = self.mate(d)
            self.copy(block, self.partner, self.handed.at[d]).wait_recv()
            self.copy(block, self.partner, self.handed.at[d]).start()

    def arrive(self):
        for d in range(self.n // 2):
            block = lax.rem(self.partner + 2 * d, self.n)
            self.copy(block, self.partner, self.send.at[0]).wait_recv()

    def drain(self):
        for d in range(1, self.n // 2):
            self.copy(self.me, self.mate(d), self.send.at[d]).wait_send()
            self.copy(self.mate(d), self.partner, self.handed.at[d]).wait_send()
        self.copy(self.me, self.partner, self.send.at[0]).wait_send()


def kernel(
    n_row,
    n_col,
    tokens_ref,
    single_ref,
    ada_gain_ref,
    scale_b_ref,
    query_b_ref,
    gate_b_ref,
    pair_gain_ref,
    pair_proj_ref,
    scale_w_hbm,
    shift_w_hbm,
    pair_hbm,
    qkvg_hbm,
    gate_w_hbm,
    out_w_hbm,
    trans_in_hbm,
    trans_out_hbm,
    out_ref,
    scale_w,
    shift_w,
    pair,
    qkvg,
    gate_w,
    trans_in,
    trans_out,
    out_w,
    mods0,
    mods1,
    bias_tx,
    bias_rx,
    keys,
    values,
    attended,
    terms32,
    terms_tx,
    terms_rx,
    resid_parts,
    load_sem,
    mods0_send,
    mods0_recv,
    mods1_send,
    mods1_recv,
    bias_send,
    bias_recv,
    att_send,
    att_recv,
    terms_send,
    terms_recv,
    w_send,
    w_hand,
    w_recv,
    k_send,
    k_hand,
    k_recv,
    v_send,
    v_hand,
    v_recv,
):
    row, col = lax.axis_index("row"), lax.axis_index("col")
    samples, rows, full = tokens_ref.shape
    width = qkvg.shape[2]
    size = full // H
    heads = width // size
    flat = samples * rows

    loads = {}
    for number, (name, source, target) in enumerate(
        (
            ("scale", scale_w_hbm, scale_w),
            ("shift", shift_w_hbm, shift_w),
            ("pair", pair_hbm, pair),
            ("gate", gate_w_hbm, gate_w),
            ("qkvg", qkvg_hbm, qkvg),
            ("out", out_w_hbm, out_w.at[col]),
            ("in", trans_in_hbm, trans_in),
            ("back", trans_out_hbm, trans_out),
        )
    ):
        loads[name] = pltpu.make_async_copy(source, target, load_sem.at[number])
        loads[name].start()

    mods0_x = Exchange("col", n_col, lambda t: mods0.at[col], mods0, mods0_send, mods0_recv)
    mods1_x = Exchange("col", n_col, lambda t: mods1.at[col], mods1, mods1_send, mods1_recv)
    bias_x = Exchange(
        "col", n_col, lambda t: bias_tx.at[pl.ds(t * heads, heads)], bias_rx, bias_send, bias_recv
    )
    att_x = Exchange("col", n_col, lambda t: attended.at[col], attended, att_send, att_recv)
    terms_x = Exchange("col", n_col, lambda t: terms_tx.at[t], terms_rx, terms_send, terms_recv)
    w_x = PairGather("col", n_col, out_w, w_send, w_hand, w_recv)
    k_x = PairGather("row", n_row, keys, k_send, k_hand, k_recv)
    v_x = PairGather("row", n_row, values, v_send, v_hand, v_recv)

    barrier = pltpu.get_barrier_semaphore()
    for d in range(1, n_col):
        pl.semaphore_signal(
            barrier,
            inc=1,
            device_id={"col": lax.rem(col + d, n_col)},
            device_id_type=pl.DeviceIdType.MESH,
        )
    for target in [k_x.mate(d) for d in range(1, n_row // 2)] + [k_x.partner]:
        pl.semaphore_signal(
            barrier, inc=1, device_id={"row": target}, device_id_type=pl.DeviceIdType.MESH
        )

    base = layer_norm(single_ref[...].astype(F32))
    cond0 = (base * ada_gain_ref[0:1, :]).astype(BF16)
    cond1 = (base * ada_gain_ref[1:2, :]).astype(BF16)
    loads["scale"].wait()
    loads["shift"].wait()
    scale0 = jax.nn.sigmoid(dot(cond0, scale_w[0]) + scale_b_ref[0:1, :])
    shift0 = dot(cond0, shift_w[0])
    mods0[col] = jnp.concatenate([scale0, shift0], axis=0).astype(BF16)
    pl.semaphore_wait(barrier, n_col - 1 + n_row // 2)
    mods0_x.start()

    loads["pair"].wait()
    proj = jnp.transpose(pair_proj_ref[...])
    proj_hi = proj.astype(BF16)
    proj_lo = (proj - proj_hi.astype(F32)).astype(BF16)
    proj_both = jnp.concatenate(
        [
            jnp.concatenate([proj_hi, proj_hi], axis=1),
            jnp.concatenate([proj_lo, proj_lo], axis=1),
        ],
        axis=0,
    )
    gain = pair_gain_ref[...]

    def bias_step(step, carry):
        first = pl.multiple_of(step * 8, 8)
        found = []
        for k in range(8):
            normed = layer_norm(pair[first + k]) * gain
            high = normed.astype(BF16)
            low = (normed - high.astype(F32)).astype(BF16)
            both = dot_t(proj_both, jnp.concatenate([high, low], axis=1))
            found.append(both[:H] + both[H:])
        stacked = jnp.stack(found, axis=0)
        bias_tx[:, pl.ds(first, 8), :] = jnp.transpose(stacked, (1, 0, 2))
        return carry

    lax.fori_loop(0, rows // 8, bias_step, 0)
    bias_x.start()

    tokens = tokens_ref[...].astype(F32)
    tokens_normed = layer_norm(tokens)

    def across(parts, first):
        return jnp.concatenate([p[first * rows : (first + 1) * rows] for p in parts], axis=1)

    mods0_x.arrive()
    parts = [mods0[c].astype(F32) for c in range(n_col)]
    norm_in = across(parts, 0)[None] * tokens_normed + across(parts, 1)[None]
    norm_in = norm_in.reshape(flat, full).astype(BF16)
    loads["qkvg"].wait()
    keys[row] = dot(norm_in, qkvg[1]).astype(BF16)
    k_x.start()
    values[row] = dot(norm_in, qkvg[2]).astype(BF16)
    v_x.start()

    loads["gate"].wait()
    gate0 = jax.nn.sigmoid(dot(cond0, gate_w[0]) + gate_b_ref[0:1, :])
    scale1 = jax.nn.sigmoid(dot(cond1, scale_w[1]) + scale_b_ref[1:2, :])
    shift1 = dot(cond1, shift_w[1])
    mods1[col] = jnp.concatenate([gate0, scale1, shift1], axis=0)
    mods1_x.start()
    loads["out"].wait()
    w_x.start()

    query = (dot(norm_in, qkvg[0]) + query_b_ref[...]).astype(BF16).astype(F32)
    gates = jax.nn.sigmoid(dot(norm_in, qkvg[3]))
    gate1 = jax.nn.sigmoid(dot(cond1, gate_w[1]) + gate_b_ref[1:2, :])
    lane = lax.broadcasted_iota(jnp.int32, (rows, width), 1)
    masks = [(lane >= h * size) & (lane < (h + 1) * size) for h in range(heads)]
    bias_rx[col] = bias_tx[pl.ds(col * heads, heads)]
    bias_x.arrive()

    k_x.hand_on()
    v_x.hand_on()
    w_x.hand_on()
    k_x.arrive()
    per_block = n_row // n_col
    weights, totals = [], []
    for s in range(samples):
        span = slice(s * rows, (s + 1) * rows)
        stacked_query = jnp.concatenate(
            [jnp.where(mask, query[span], 0.0) for mask in masks], axis=0
        ).astype(BF16)
        scores = []
        for b in range(n_col):
            block = jnp.concatenate(
                [keys[b * per_block + r].astype(F32)[span] for r in range(per_block)], axis=0
            ).astype(BF16)
            bias = bias_rx[b].reshape(heads * rows, per_block * rows)
            scores.append(dot_t(stacked_query, block) * (1.0 / math.sqrt(size)) + bias)
        peak = functools.reduce(jnp.maximum, scores)
        peak = jnp.max(peak, axis=-1, keepdims=True)
        scores = [jnp.exp(score - peak) for score in scores]
        totals.append(jnp.sum(functools.reduce(jnp.add, scores), axis=-1, keepdims=True))
        weights.append([score.astype(BF16) for score in scores])

    v_x.arrive()
    results = []
    for s in range(samples):
        span = slice(s * rows, (s + 1) * rows)
        accum = jnp.zeros((heads * rows, width), F32)
        for b in range(n_col):
            block = jnp.concatenate(
                [values[b * per_block + r].astype(F32)[span] for r in range(per_block)], axis=0
            ).astype(BF16)
            accum = accum + dot(weights[s][b], block)
        accum = accum / totals[s]
        mine = jnp.zeros((rows, width), F32)
        for h in range(heads):
            mine = jnp.where(masks[h], accum[h * rows : (h + 1) * rows], mine)
        results.append(gates[span] * mine)
    attended[col] = jnp.concatenate(results, axis=0).astype(BF16)
    att_x.start()

    mods1_x.arrive()
    parts = [mods1[c] for c in range(n_col)]
    gate0_all, scale1_all, shift1_all = (across(parts, k)[None] for k in range(3))
    w_x.arrive()
    att_x.arrive()
    projected = jnp.zeros((flat, full), F32)
    for c in range(n_col):
        projected = projected + dot(attended[c], out_w[c])
    resid = tokens + gate0_all * projected.reshape(samples, rows, full)
    middle = (scale1_all * layer_norm(resid) + shift1_all).reshape(flat, full).astype(BF16)
    loads["in"].wait()
    inner = dot(middle, trans_in[0])
    hidden = (jax.nn.silu(inner) * dot(middle, trans_in[1])).astype(BF16)
    loads["back"].wait()
    terms = dot(hidden, trans_out[...])
    for c in range(n_col):
        part = terms[:, c * width : (c + 1) * width]
        terms32[c] = part
        terms_tx[c] = part.astype(BF16)
    terms_x.start()
    resid = resid.reshape(flat, full)
    for c in range(n_col):
        resid_parts[c] = resid[:, c * width : (c + 1) * width]
    outward = terms32[col]
    terms_x.arrive()
    for d in range(1, n_col):
        outward = outward + terms_rx[lax.rem(col + d, n_col)].astype(F32)
    outward = outward.reshape(samples, rows, width)
    mixed = resid_parts[col].reshape(samples, rows, width) + gate1[None] * outward
    out_ref[...] = mixed.astype(BF16)

    for exchange in (mods0_x, bias_x, mods1_x, w_x, k_x, v_x, att_x, terms_x):
        exchange.drain()


def shards(
    n_row,
    n_col,
    tokens,
    single_cond,
    pair_cond,
    ada_gain,
    ada_scale_w,
    ada_scale_b,
    adaptive_shift_weight,
    pair_gain,
    pair_proj,
    qkvg_weight,
    query_bias,
    output_weight,
    out_gate_w,
    out_gate_b,
    transition_input_weight,
    trans_out,
):
    samples, rows, full = tokens.shape
    width = qkvg_weight.shape[2]
    heads = width * H // full
    flat = samples * rows
    keys_here = pair_cond.shape[1]
    vmem = pl.BlockSpec(memory_space=pltpu.VMEM)
    hbm = pl.BlockSpec(memory_space=pl.ANY)

    def like(array):
        return pltpu.VMEM(array.shape, array.dtype)

    def sems(n):
        return pltpu.SemaphoreType.DMA((n,))

    return pl.pallas_call(
        functools.partial(kernel, n_row, n_col),
        out_shape=jax.ShapeDtypeStruct((samples, rows, width), BF16),
        in_specs=[vmem] * 8 + [hbm] * 8,
        out_specs=vmem,
        scratch_shapes=[
            like(ada_scale_w),
            like(adaptive_shift_weight),
            like(pair_cond),
            like(qkvg_weight),
            like(out_gate_w),
            like(transition_input_weight),
            like(trans_out),
            pltpu.VMEM((n_col,) + output_weight.shape, BF16),
            pltpu.VMEM((n_col, 2 * rows, width), BF16),
            pltpu.VMEM((n_col, 3 * rows, width), F32),
            pltpu.VMEM((H, rows, keys_here), F32),
            pltpu.VMEM((n_col, heads, rows, keys_here), F32),
            pltpu.VMEM((n_row, flat, width), BF16),
            pltpu.VMEM((n_row, flat, width), BF16),
            pltpu.VMEM((n_col, flat, width), BF16),
            pltpu.VMEM((n_col, flat, width), F32),
            pltpu.VMEM((n_col, flat, width), BF16),
            pltpu.VMEM((n_col, flat, width), BF16),
            pltpu.VMEM((n_col, flat, width), F32),
            sems(8),
        ]
        + [sems(n_col)] * 10
        + [sems(n_col)] * 3
        + [sems(n_row)] * 6,
        compiler_params=pltpu.CompilerParams(
            collective_id=0, has_side_effects=True, vmem_limit_bytes=56 * 1024 * 1024
        ),
    )(
        tokens,
        single_cond,
        ada_gain,
        ada_scale_b,
        query_bias[None],
        out_gate_b,
        pair_gain[None],
        pair_proj,
        ada_scale_w,
        adaptive_shift_weight,
        pair_cond,
        qkvg_weight,
        out_gate_w,
        output_weight,
        transition_input_weight,
        trans_out,
    )


def solution(mesh):
    return jax.shard_map(
        functools.partial(shards, mesh.shape["row"], mesh.shape["col"]),
        mesh=mesh,
        in_specs=(
            P(None, "row", None),
            P("row", None),
            P("row", "col", None),
            P(),
            P(None, None, "col"),
            P(None, "col"),
            P(None, None, "col"),
            P(),
            P(),
            P(None, None, "col"),
            P("col"),
            P("col", None),
            P(None, None, "col"),
            P(None, "col"),
            P(None, None, "col"),
            P("col", None),
        ),
        out_specs=P(None, "row", "col"),
        check_vma=False,
    )
```

time: 196 us -> 55.3 us (0.28)
  blocking collectives: 71.8 us -> 0 us
  waiting for transfers between devices: 68.4 us -> 0 us
  Pallas kernels: 0 us -> 45.7 us
  between operations: 13.9 us -> 0.01 us
  matrix products: 13.6 us -> 0 us
  other arithmetic: 6.79 us -> 0 us
  local copies, waits for them, and re-layouts: 14.7 us -> 9.34 us
  starting transfers between devices: 4.95 us -> 0 us
    all_gather x3 -> x0, blocking collectives: 71.8 us -> none  [the longest x1 25.7 us: shards(): value_piece = lax.all_gather(value_rows, 'row', axis=1, tiled=True)]
    pallas_call x0 -> x1, Pallas kernels: none -> 45.7 us  [shards(): pl.pallas_call(functools.partial(kernel, n_row, n_col), out_shape=jax.Sha...]
    psum x1 -> x0, waiting for transfers between devices: 45 us -> none  [shards(): projected_output = lax.psum(partial_terms, 'col')]
    unnamed x3 -> x0, waiting for transfers between devices: 23.4 us -> none
    dot_general x13 -> x0, matrix products: 13.6 us -> none  [the longest x1 4.34 us: shards(): jnp.einsum('ijc,ch->hij', pair_normed, pair_proj, precision=lax.Precision...]
    reduce_sum x9 -> x0, other arithmetic: 5.87 us -> none  [the longest x4 3.73 us: layer_norm(): center = values - jnp.mean(values, axis=-1, keepdims=True)]
    all_to_all x1 -> x0, starting transfers between devices: 4.73 us -> none  [shards(): lax.all_to_all(bias, 'col', split_axis=0, concat_axis=2, tiled=True)]
    unnamed x44 -> x10, local copies, waits for them, and re-layouts: 4.96 us -> 9.34 us
  transfers between devices with their start and end apart: 3 -> 0, of which waited for: 2 -> 0; matrix products, arithmetic and copies ran while one was open for 6% -> 0% of each run, Pallas kernels for 0% -> 0%
where the time goes in v1:
time: 55.3 us; the launch traced here: 55.1 us
  Pallas kernels  45.7 us (83%)
  local copies, waits for them, and re-layouts  9.34 us (17%)
    pallas_call x1, Pallas kernels, shards(): pl.pallas_call(functools.partial(kernel, n_row, n_col), out_shape=jax.Sha...  45.7 us
    unnamed x10, local copies, waits for them, and re-layouts  9.34 us

profile of v1, /device:TPU:9, one launch (start us, length us, event | category | flops | bytes accessed | tf_op | source)
XLA Modules:
  0.0 55.1 jit_solution(5339578278256601547)
XLA Ops:
  0.0 0.0 copy-start.1
  0.0 0.0 copy-start
  0.0 1.5 %copy.17.pair_proj_ref = f32[128,16]{1,0:T(8,128)} copy(f32[128,16]{0,1:T(8,128)} %param.24) | data formatting | bytes 16384 | tf_op args[8]
  1.5 1.9 %copy.18.scale_w_hbm = bf16[2,384,192]{2,1,0:T(8,128)(2,1)} copy(bf16[2,384,192]{1,2,0:T(8,128)(2,1)} %param.20) | data formatting | bytes 589824 | tf_op args[4]
  3.4 1.9 %copy.19.shift_w_hbm = bf16[2,384,192]{2,1,0:T(8,128)(2,1)} copy(bf16[2,384,192]{1,2,0:T(8,128)(2,1)} %param.22) | data formatting | bytes 589824 | tf_op args[6]
  5.3 0.0 copy-done.1
  5.3 0.9 %copy.21.gate_w_hbm = bf16[2,384,192]{2,1,0:T(8,128)(2,1)} copy(bf16[2,384,192]{1,2,0:T(8,128)(2,1)S(1)} %copy-done.1) | data formatting | bytes 589824 | tf_op args[12]
  6.3 0.0 copy-done
  6.3 1.5 %copy.20.qkvg_hbm = bf16[4,768,192]{2,1,0:T(8,128)(2,1)} copy(bf16[4,768,192]{1,2,0:T(8,128)(2,1)S(1)} %copy-done) | data formatting | bytes 2359296 | tf_op args[9]
  7.8 45.7 %shard_map.154 = bf16[4,40,192]{2,1,0:T(8,128)(2,1)} custom-call(bf16[4,40,768]{2,1,0:T(8,128)(2,1)} %tokens_ref.1, bf16[40,384]{1,0:T(8,128)(2,1)} %single_ref.1, f32[2,384]{1,0:T(2,128)} %ada_gain_ref.1, f32[2,192]{1,0:T(2,128)} %scale_b_ref.1, f32[1,192]{1,0:T(1,128)} %bitcast.2, f32[2,192]{1,0:T(2,128)} %gate_b_ref.1, f32[1,128]{1,0:T(1,128)} %bitcast.3, ...), custom_call_target="tpu_custom_call" | custom-call | tf_op jit(solution)/shard_map/pallas_call | solution.py:403
  53.5 1.5 %copy.23 = bf16[4,40,192]{2,1,0:T(8,128)(2,1)} copy(bf16[4,40,192]{2,1,0:T(8,128)(2,1)} %shard_map.154) | data formatting | bytes 122880
Async XLA Ops:
  0.0 5.3 %copy-start.1 = (bf16[2,384,192]{1,2,0:T(8,128)(2,1)S(1)}, bf16[2,384,192]{1,2,0:T(8,128)(2,1)}, u32[]{:S(2)}) copy-start(bf16[2,384,192]{1,2,0:T(8,128)(2,1)} %param.28) | copy-start | bytes 884740
  0.0 6.3 %copy-start = (bf16[4,768,192]{1,2,0:T(8,128)(2,1)S(1)}, bf16[4,768,192]{1,2,0:T(8,128)(2,1)}, u32[]{:S(2)}) copy-start(bf16[4,768,192]{1,2,0:T(8,128)(2,1)} %param.25) | copy-start | bytes 3538948

commit v2 on v1

--- a/solution.py
+++ b/solution.py
@@ -171,7 +171,7 @@
 ):
     row, col = lax.axis_index("row"), lax.axis_index("col")
     samples, rows, full = tokens_ref.shape
-    width = qkvg.shape[2]
+    width = qkvg.shape[1]
     size = full // H
     heads = width // size
     flat = samples * rows
@@ -221,14 +221,14 @@
     cond1 = (base * ada_gain_ref[1:2, :]).astype(BF16)
     loads["scale"].wait()
     loads["shift"].wait()
-    scale0 = jax.nn.sigmoid(dot(cond0, scale_w[0]) + scale_b_ref[0:1, :])
-    shift0 = dot(cond0, shift_w[0])
+    scale0 = jax.nn.sigmoid(dot_t(cond0, scale_w[0]) + scale_b_ref[0:1, :])
+    shift0 = dot_t(cond0, shift_w[0])
     mods0[col] = jnp.concatenate([scale0, shift0], axis=0).astype(BF16)
     pl.semaphore_wait(barrier, n_col - 1 + n_row // 2)
     mods0_x.start()
 
     loads["pair"].wait()
-    proj = jnp.transpose(pair_proj_ref[...])
+    proj = pair_proj_ref[...]
     proj_hi = proj.astype(BF16)
     proj_lo = (proj - proj_hi.astype(F32)).astype(BF16)
     proj_both = jnp.concatenate(
@@ -267,23 +267,23 @@
     norm_in = across(parts, 0)[None] * tokens_normed + across(parts, 1)[None]
     norm_in = norm_in.reshape(flat, full).astype(BF16)
     loads["qkvg"].wait()
-    keys[row] = dot(norm_in, qkvg[1]).astype(BF16)
+    keys[row] = dot_t(norm_in, qkvg[1]).astype(BF16)
     k_x.start()
-    values[row] = dot(norm_in, qkvg[2]).astype(BF16)
+    values[row] = dot_t(norm_in, qkvg[2]).astype(BF16)
     v_x.start()
 
     loads["gate"].wait()
-    gate0 = jax.nn.sigmoid(dot(cond0, gate_w[0]) + gate_b_ref[0:1, :])
-    scale1 = jax.nn.sigmoid(dot(cond1, scale_w[1]) + scale_b_ref[1:2, :])
-    shift1 = dot(cond1, shift_w[1])
+    gate0 = jax.nn.sigmoid(dot_t(cond0, gate_w[0]) + gate_b_ref[0:1, :])
+    scale1 = jax.nn.sigmoid(dot_t(cond1, scale_w[1]) + scale_b_ref[1:2, :])
+    shift1 = dot_t(cond1, shift_w[1])
     mods1[col] = jnp.concatenate([gate0, scale1, shift1], axis=0)
     mods1_x.start()
     loads["out"].wait()
     w_x.start()
 
-    query = (dot(norm_in, qkvg[0]) + query_b_ref[...]).astype(BF16).astype(F32)
-    gates = jax.nn.sigmoid(dot(norm_in, qkvg[3]))
-    gate1 = jax.nn.sigmoid(dot(cond1, gate_w[1]) + gate_b_ref[1:2, :])
+    query = (dot_t(norm_in, qkvg[0]) + query_b_ref[...]).astype(BF16).astype(F32)
+    gates = jax.nn.sigmoid(dot_t(norm_in, qkvg[3]))
+    gate1 = jax.nn.sigmoid(dot_t(cond1, gate_w[1]) + gate_b_ref[1:2, :])
     lane = lax.broadcasted_iota(jnp.int32, (rows, width), 1)
     masks = [(lane >= h * size) & (lane < (h + 1) * size) for h in range(heads)]
     bias_rx[col] = bias_tx[pl.ds(col * heads, heads)]
@@ -360,7 +360,7 @@
         outward = outward + terms_rx[lax.rem(col + d, n_col)].astype(F32)
     outward = outward.reshape(samples, rows, width)
     mixed = resid_parts[col].reshape(samples, rows, width) + gate1[None] * outward
-    out_ref[...] = mixed.astype(BF16)
+    out_ref[...] = mixed
 
     for exchange in (mods0_x, bias_x, mods1_x, w_x, k_x, v_x, att_x, terms_x):
         exchange.drain()
@@ -391,6 +391,10 @@
     heads = width * H // full
     flat = samples * rows
     keys_here = pair_cond.shape[1]
+    ada_scale_w, adaptive_shift_weight, qkvg_weight, out_gate_w = (
+        jnp.swapaxes(array, 1, 2)
+        for array in (ada_scale_w, adaptive_shift_weight, qkvg_weight, out_gate_w)
+    )
     vmem = pl.BlockSpec(memory_space=pltpu.VMEM)
     hbm = pl.BlockSpec(memory_space=pl.ANY)
 
@@ -400,9 +404,9 @@
     def sems(n):
         return pltpu.SemaphoreType.DMA((n,))
 
-    return pl.pallas_call(
+    mixed = pl.pallas_call(
         functools.partial(kernel, n_row, n_col),
-        out_shape=jax.ShapeDtypeStruct((samples, rows, width), BF16),
+        out_shape=jax.ShapeDtypeStruct((samples, rows, width), F32),
         in_specs=[vmem] * 8 + [hbm] * 8,
         out_specs=vmem,
         scratch_shapes=[
@@ -441,7 +445,7 @@
         query_bias[None],
         out_gate_b,
         pair_gain[None],
-        pair_proj,
+        pair_proj.T,
         ada_scale_w,
         adaptive_shift_weight,
         pair_cond,
@@ -451,6 +455,7 @@
         transition_input_weight,
         trans_out,
     )
+    return mixed.astype(BF16)
 
 
 def solution(mesh):

time: 55.3 us -> 47.5 us (0.86)
  local copies, waits for them, and re-layouts: 9.34 us -> 0 us
  other arithmetic: 0 us -> 1.56 us
    unnamed x10 -> x0, local copies, waits for them, and re-layouts: 9.34 us -> none
    convert_element_type x0 -> x1, other arithmetic: none -> 1.56 us  [shards(): return mixed.astype(BF16)]
where the time goes in v2:
time: 47.5 us; the launch traced here: 47.4 us
  Pallas kernels  45.8 us (96%)
  other arithmetic  1.56 us (3%)
    pallas_call x1, Pallas kernels, shards(): pl.pallas_call(functools.partial(kernel, n_row, n_col), out_shape=jax.Sha...  45.8 us
    convert_element_type x1, other arithmetic, shards(): return mixed.astype(BF16)  1.56 us

profile of v2, /device:TPU:9, one launch (start us, length us, event | category | flops | bytes accessed | tf_op | source)
XLA Modules:
  0.0 47.4 jit_solution(4518983993503122189)
XLA Ops:
  0.0 45.8 %shard_map.154 = f32[4,40,192]{2,1,0:T(8,128)} custom-call(bf16[4,40,768]{2,1,0:T(8,128)(2,1)} %tokens_ref.1, bf16[40,384]{1,0:T(8,128)(2,1)} %single_ref.1, f32[2,384]{1,0:T(2,128)} %ada_gain_ref.1, f32[2,192]{1,0:T(2,128)} %scale_b_ref.1, f32[1,192]{1,0:T(1,128)} %bitcast.12, f32[2,192]{1,0:T(2,128)} %gate_b_ref.1, f32[1,128]{1,0:T(1,128)} %bitcast.13, ...), custom_call_target="tpu_custom_call" | custom-call | tf_op jit(solution)/shard_map/pallas_call | solution.py:407
  45.8 1.6 %convert_element_type.3 = bf16[4,40,192]{2,1,0:T(8,128)(2,1)} convert(f32[4,40,192]{2,1,0:T(8,128)} %shard_map.154) | non-fusion elementwise | flops 30720 | bytes 184320 | tf_op jit(solution)/shard_map/convert_element_type | solution.py:458

commit v3 on v2

--- a/solution.py
+++ b/solution.py
@@ -9,6 +9,7 @@
 from jax.sharding import PartitionSpec as P
 
 H = 16
+PARTS = 2
 epsilon = 1e-05
 F32 = jnp.float32
 BF16 = jnp.bfloat16
@@ -107,6 +108,74 @@
             self.copy(self.me, self.mate(d), self.send.at[d]).wait_send()
             self.copy(self.mate(d), self.partner, self.handed.at[d]).wait_send()
         self.copy(self.me, self.partner, self.send.at[0]).wait_send()
+
+
+class LineGather:
+    def __init__(self, axis, n, buffer, send, handed, recv):
+        self.axis, self.n, self.buffer = axis, n, buffer
+        self.send, self.handed, self.recv = send, handed, recv
+        self.me = lax.axis_index(axis)
+        self.side = lax.rem(self.me, 2)
+        self.place = self.me // 2
+        self.length = n // 2
+        self.partner = self.me + 1 - 2 * self.side
+
+    def copy(self, block, target, sem):
+        return pltpu.make_async_remote_copy(
+            src_ref=self.buffer.at[block],
+            dst_ref=self.buffer.at[block],
+            send_sem=sem,
+            recv_sem=self.recv.at[block],
+            device_id={self.axis: target},
+            device_id_type=pl.DeviceIdType.MESH,
+        )
+
+    def upward(self, k):
+        return self.copy(self.me - 2 * k, self.me + 2, self.send.at[k])
+
+    def downward(self, k):
+        return self.copy(self.me + 2 * k, self.me - 2, self.send.at[self.length + k])
+
+    def from_below(self, k):
+        return self.copy(self.me - 2 * k, self.partner, self.handed.at[k])
+
+    def from_above(self, k):
+        return self.copy(self.me + 2 * k, self.partner, self.handed.at[self.length + k])
+
+    def start(self):
+        pl.when(self.place < self.length - 1)(lambda: self.upward(0).start())
+        pl.when(self.place > 0)(lambda: self.downward(0).start())
+        self.from_below(0).start()
+
+    def step(self, k):
+        @pl.when(self.place >= k)
+        def _():
+            self.from_below(k).wait_recv()
+            pl.when(self.place < self.length - 1)(lambda: self.upward(k).start())
+            self.from_below(k).start()
+
+        @pl.when(self.place < self.length - k)
+        def _():
+            self.from_above(k).wait_recv()
+            pl.when(self.place > 0)(lambda: self.downward(k).start())
+            self.from_above(k).start()
+
+    def arrive(self):
+        for d in range(self.length):
+            self.copy(2 * d + 1 - self.side, self.partner, self.send.at[0]).wait_recv()
+
+    def drain(self):
+        self.from_below(0).wait_send()
+        for k in range(self.length):
+            below = self.place >= k
+            above = self.place < self.length - k
+            last = self.place == self.length - 1
+            first = self.place == 0
+            pl.when(below & ~last)(lambda k=k: self.upward(k).wait_send())
+            pl.when(above & ~first)(lambda k=k: self.downward(k).wait_send())
+            if k:
+                pl.when(below)(lambda k=k: self.from_below(k).wait_send())
+                pl.when(above)(lambda k=k: self.from_above(k).wait_send())
 
 
 def kernel(
@@ -141,8 +210,7 @@
     mods1,
     bias_tx,
     bias_rx,
-    keys,
-    values,
+    kv,
     attended,
     terms32,
     terms_tx,
@@ -162,12 +230,9 @@
     w_send,
     w_hand,
     w_recv,
-    k_send,
-    k_hand,
-    k_recv,
-    v_send,
-    v_hand,
-    v_recv,
+    kv_send,
+    kv_hand,
+    kv_recv,
 ):
     row, col = lax.axis_index("row"), lax.axis_index("col")
     samples, rows, full = tokens_ref.shape
@@ -175,6 +240,8 @@
     size = full // H
     heads = width // size
     flat = samples * rows
+    some = samples // PARTS
+    part_flat = flat // PARTS
 
     loads = {}
     for number, (name, source, target) in enumerate(
@@ -200,8 +267,10 @@
     att_x = Exchange("col", n_col, lambda t: attended.at[col], attended, att_send, att_recv)
     terms_x = Exchange("col", n_col, lambda t: terms_tx.at[t], terms_rx, terms_send, terms_recv)
     w_x = PairGather("col", n_col, out_w, w_send, w_hand, w_recv)
-    k_x = PairGather("row", n_row, keys, k_send, k_hand, k_recv)
-    v_x = PairGather("row", n_row, values, v_send, v_hand, v_recv)
+    kv_x = [
+        LineGather("row", n_row, kv.at[g], kv_send.at[g], kv_hand.at[g], kv_recv.at[g])
+        for g in range(PARTS)
+    ]
 
     barrier = pltpu.get_barrier_semaphore()
     for d in range(1, n_col):
@@ -211,7 +280,7 @@
             device_id={"col": lax.rem(col + d, n_col)},
             device_id_type=pl.DeviceIdType.MESH,
         )
-    for target in [k_x.mate(d) for d in range(1, n_row // 2)] + [k_x.partner]:
+    for target in [lax.rem(row + 2 * d, n_row) for d in range(1, n_row // 2)] + [kv_x[0].partner]:
         pl.semaphore_signal(
             barrier, inc=1, device_id={"row": target}, device_id_type=pl.DeviceIdType.MESH
         )
@@ -267,16 +336,19 @@
     norm_in = across(parts, 0)[None] * tokens_normed + across(parts, 1)[None]
     norm_in = norm_in.reshape(flat, full).astype(BF16)
     loads["qkvg"].wait()
-    keys[row] = dot_t(norm_in, qkvg[1]).astype(BF16)
-    k_x.start()
-    values[row] = dot_t(norm_in, qkvg[2]).astype(BF16)
-    v_x.start()
+    key = dot_t(norm_in, qkvg[1])
+    value = dot_t(norm_in, qkvg[2])
+    for g in range(PARTS):
+        span = slice(g * part_flat, (g + 1) * part_flat)
+        kv[g, row] = jnp.concatenate([key[span], value[span]], axis=1).astype(BF16)
+    kv_x[0].start()
 
     loads["gate"].wait()
     gate0 = jax.nn.sigmoid(dot_t(cond0, gate_w[0]) + gate_b_ref[0:1, :])
     scale1 = jax.nn.sigmoid(dot_t(cond1, scale_w[1]) + scale_b_ref[1:2, :])
     shift1 = dot_t(cond1, shift_w[1])
-    mods1[col] = jnp.concatenate([gate0, scale1, shift1], axis=0)
+    fill = jnp.zeros((mods1.shape[1] - 3 * rows, width), F32)
+    mods1[col] = jnp.concatenate([gate0, scale1, shift1, fill], axis=0).astype(BF16)
     mods1_x.start()
     loads["out"].wait()
     w_x.start()
@@ -288,66 +360,85 @@
     masks = [(lane >= h * size) & (lane < (h + 1) * size) for h in range(heads)]
     bias_rx[col] = bias_tx[pl.ds(col * heads, heads)]
     bias_x.arrive()
-
-    k_x.hand_on()
-    v_x.hand_on()
+    per_block = n_row // n_col
+
+    half = flat // 2
+
+    def pack(array):
+        return jnp.concatenate([array[:half], array[half:]], axis=1)
+
+    def unpack(array):
+        return jnp.concatenate([array[:, :width], array[:, width:]], axis=0)
+
+    def tokens_of(g, which, b, s):
+        lanes = slice(which * width, (which + 1) * width)
+        return jnp.concatenate(
+            [
+                kv[g, b * per_block + r].astype(F32)[s * rows : (s + 1) * rows, lanes]
+                for r in range(per_block)
+            ],
+            axis=0,
+        ).astype(BF16)
+
+    def attend(g):
+        results = []
+        for s in range(some):
+            span = slice((g * some + s) * rows, (g * some + s + 1) * rows)
+            stacked_query = jnp.concatenate(
+                [jnp.where(mask, query[span], 0.0) for mask in masks], axis=0
+            ).astype(BF16)
+            scores = []
+            for b in range(n_col):
+                bias = bias_rx[b].reshape(heads * rows, per_block * rows)
+                score = dot_t(stacked_query, tokens_of(g, 0, b, s))
+                scores.append(score * (1.0 / math.sqrt(size)) + bias)
+            peak = functools.reduce(jnp.maximum, scores)
+            peak = jnp.max(peak, axis=-1, keepdims=True)
+            scores = [jnp.exp(score - peak) for score in scores]
+            total = jnp.sum(functools.reduce(jnp.add, scores), axis=-1, keepdims=True)
+            accum = jnp.zeros((heads * rows, width), F32)
+            for b in range(n_col):
+                accum = accum + dot(scores[b].astype(BF16), tokens_of(g, 1, b, s))
+            accum = accum / total
+            mine = jnp.zeros((rows, width), F32)
+            for h in range(heads):
+                mine = jnp.where(masks[h], accum[h * rows : (h + 1) * rows], mine)
+            results.append(gates[span] * mine)
+        return results
+
+    first, second = kv_x
+    steps = n_row // 2
+    for k in range(1, steps):
+        first.step(k)
+        if k == 1:
+            second.start()
+        else:
+            second.step(k - 1)
+    second.step(steps - 1)
     w_x.hand_on()
-    k_x.arrive()
-    per_block = n_row // n_col
-    weights, totals = [], []
-    for s in range(samples):
-        span = slice(s * rows, (s + 1) * rows)
-        stacked_query = jnp.concatenate(
-            [jnp.where(mask, query[span], 0.0) for mask in masks], axis=0
-        ).astype(BF16)
-        scores = []
-        for b in range(n_col):
-            block = jnp.concatenate(
-                [keys[b * per_block + r].astype(F32)[span] for r in range(per_block)], axis=0
-            ).astype(BF16)
-            bias = bias_rx[b].reshape(heads * rows, per_block * rows)
-            scores.append(dot_t(stacked_query, block) * (1.0 / math.sqrt(size)) + bias)
-        peak = functools.reduce(jnp.maximum, scores)
-        peak = jnp.max(peak, axis=-1, keepdims=True)
-        scores = [jnp.exp(score - peak) for score in scores]
-        totals.append(jnp.sum(functools.reduce(jnp.add, scores), axis=-1, keepdims=True))
-        weights.append([score.astype(BF16) for score in scores])
-
-    v_x.arrive()
-    results = []
-    for s in range(samples):
-        span = slice(s * rows, (s + 1) * rows)
-        accum = jnp.zeros((heads * rows, width), F32)
-        for b in range(n_col):
-            block = jnp.concatenate(
-                [values[b * per_block + r].astype(F32)[span] for r in range(per_block)], axis=0
-            ).astype(BF16)
-            accum = accum + dot(weights[s][b], block)
-        accum = accum / totals[s]
-        mine = jnp.zeros((rows, width), F32)
-        for h in range(heads):
-            mine = jnp.where(masks[h], accum[h * rows : (h + 1) * rows], mine)
-        results.append(gates[span] * mine)
-    attended[col] = jnp.concatenate(results, axis=0).astype(BF16)
+    first.arrive()
+    results = attend(0)
+    second.arrive()
+    results = results + attend(1)
+    attended[col] = pack(jnp.concatenate(results, axis=0)).astype(BF16)
     att_x.start()
-
     mods1_x.arrive()
-    parts = [mods1[c] for c in range(n_col)]
+    parts = [mods1[c].astype(F32) for c in range(n_col)]
     gate0_all, scale1_all, shift1_all = (across(parts, k)[None] for k in range(3))
     w_x.arrive()
+    loads["in"].wait()
+    loads["back"].wait()
     att_x.arrive()
     projected = jnp.zeros((flat, full), F32)
     for c in range(n_col):
-        projected = projected + dot(attended[c], out_w[c])
+        projected = projected + dot(unpack(attended[c].astype(F32)).astype(BF16), out_w[c])
     resid = tokens + gate0_all * projected.reshape(samples, rows, full)
     middle = (scale1_all * layer_norm(resid) + shift1_all).reshape(flat, full).astype(BF16)
-    loads["in"].wait()
     inner = dot(middle, trans_in[0])
     hidden = (jax.nn.silu(inner) * dot(middle, trans_in[1])).astype(BF16)
-    loads["back"].wait()
     terms = dot(hidden, trans_out[...])
     for c in range(n_col):
-        part = terms[:, c * width : (c + 1) * width]
+        part = pack(terms[:, c * width : (c + 1) * width])
         terms32[c] = part
         terms_tx[c] = part.astype(BF16)
     terms_x.start()
@@ -358,11 +449,11 @@
     terms_x.arrive()
     for d in range(1, n_col):
         outward = outward + terms_rx[lax.rem(col + d, n_col)].astype(F32)
-    outward = outward.reshape(samples, rows, width)
+    outward = unpack(outward).reshape(samples, rows, width)
     mixed = resid_parts[col].reshape(samples, rows, width) + gate1[None] * outward
     out_ref[...] = mixed
 
-    for exchange in (mods0_x, bias_x, mods1_x, w_x, k_x, v_x, att_x, terms_x):
+    for exchange in [mods0_x, bias_x, mods1_x, w_x, att_x, terms_x] + kv_x:
         exchange.drain()
 
 
@@ -401,8 +492,8 @@
     def like(array):
         return pltpu.VMEM(array.shape, array.dtype)
 
-    def sems(n):
-        return pltpu.SemaphoreType.DMA((n,))
+    def sems(*shape):
+        return pltpu.SemaphoreType.DMA(shape)
 
     mixed = pl.pallas_call(
         functools.partial(kernel, n_row, n_col),
@@ -419,21 +510,19 @@
             like(trans_out),
             pltpu.VMEM((n_col,) + output_weight.shape, BF16),
             pltpu.VMEM((n_col, 2 * rows, width), BF16),
-            pltpu.VMEM((n_col, 3 * rows, width), F32),
+            pltpu.VMEM((n_col, -(-3 * rows // 16) * 16, width), BF16),
             pltpu.VMEM((H, rows, keys_here), F32),
             pltpu.VMEM((n_col, heads, rows, keys_here), F32),
-            pltpu.VMEM((n_row, flat, width), BF16),
-            pltpu.VMEM((n_row, flat, width), BF16),
-            pltpu.VMEM((n_col, flat, width), BF16),
-            pltpu.VMEM((n_col, flat, width), F32),
-            pltpu.VMEM((n_col, flat, width), BF16),
-            pltpu.VMEM((n_col, flat, width), BF16),
+            pltpu.VMEM((PARTS, n_row, flat // PARTS, 2 * width), BF16),
+            pltpu.VMEM((n_col, flat // 2, 2 * width), BF16),
+            pltpu.VMEM((n_col, flat // 2, 2 * width), F32),
+            pltpu.VMEM((n_col, flat // 2, 2 * width), BF16),
+            pltpu.VMEM((n_col, flat // 2, 2 * width), BF16),
             pltpu.VMEM((n_col, flat, width), F32),
             sems(8),
         ]
-        + [sems(n_col)] * 10
-        + [sems(n_col)] * 3
-        + [sems(n_row)] * 6,
+        + [sems(n_col)] * 13
+        + [sems(PARTS, n_row)] * 3,
         compiler_params=pltpu.CompilerParams(
             collective_id=0, has_side_effects=True, vmem_limit_bytes=56 * 1024 * 1024
         ),

time: 47.5 us -> 42.6 us (0.90)
  the two profiles are of different devices: /device:TPU:9 before, /device:TPU:1 now
where the time goes in v3:
time: 42.6 us; the launch traced here: 42.4 us
  Pallas kernels  40.9 us (96%)
  other arithmetic  1.56 us (4%)
    pallas_call x1, Pallas kernels, shards(): pl.pallas_call(functools.partial(kernel, n_row, n_col), out_shape=jax.Sha...  40.9 us
    convert_element_type x1, other arithmetic, shards(): return mixed.astype(BF16)  1.56 us

profile of v3, /device:TPU:1, one launch (start us, length us, event | category | flops | bytes accessed | tf_op | source)
XLA Modules:
  0.0 42.4 jit_solution(5234097256372761469)
XLA Ops:
  0.0 40.9 %shard_map.154 = f32[4,40,192]{2,1,0:T(8,128)} custom-call(bf16[4,40,768]{2,1,0:T(8,128)(2,1)} %tokens_ref.1, bf16[40,384]{1,0:T(8,128)(2,1)} %single_ref.1, f32[2,384]{1,0:T(2,128)} %ada_gain_ref.1, f32[2,192]{1,0:T(2,128)} %scale_b_ref.1, f32[1,192]{1,0:T(1,128)} %bitcast.12, f32[2,192]{1,0:T(2,128)} %gate_b_ref.1, f32[1,128]{1,0:T(1,128)} %bitcast.13, ...), custom_call_target="tpu_custom_call" | custom-call | tf_op jit(solution)/shard_map/pallas_call | solution.py:498
  40.9 1.6 %convert_element_type.3 = bf16[4,40,192]{2,1,0:T(8,128)(2,1)} convert(f32[4,40,192]{2,1,0:T(8,128)} %shard_map.154) | non-fusion elementwise | flops 30720 | bytes 184320 | tf_op jit(solution)/shard_map/convert_element_type | solution.py:547

commit v4 on v3

--- a/solution.py
+++ b/solution.py
@@ -341,7 +341,10 @@
     for g in range(PARTS):
         span = slice(g * part_flat, (g + 1) * part_flat)
         kv[g, row] = jnp.concatenate([key[span], value[span]], axis=1).astype(BF16)
-    kv_x[0].start()
+    first, second = kv_x
+    steps = n_row // 2
+    first.start()
+    second.start()
 
     loads["gate"].wait()
     gate0 = jax.nn.sigmoid(dot_t(cond0, gate_w[0]) + gate_b_ref[0:1, :])
@@ -352,6 +355,8 @@
     mods1_x.start()
     loads["out"].wait()
     w_x.start()
+    first.step(1)
+    second.step(1)
 
     query = (dot_t(norm_in, qkvg[0]) + query_b_ref[...]).astype(BF16).astype(F32)
     gates = jax.nn.sigmoid(dot_t(norm_in, qkvg[3]))
@@ -406,15 +411,9 @@
             results.append(gates[span] * mine)
         return results
 
-    first, second = kv_x
-    steps = n_row // 2
-    for k in range(1, steps):
+    for k in range(2, steps):
         first.step(k)
-        if k == 1:
-            second.start()
-        else:
-            second.step(k - 1)
-    second.step(steps - 1)
+        second.step(k)
     w_x.hand_on()
     first.arrive()
     results = attend(0)

time: 42.6 us -> 38.8 us (0.911)
  Pallas kernels: 40.9 us -> 37 us
    pallas_call x1, Pallas kernels: 40.9 us -> 37 us  [shards(): pl.pallas_call(functools.partial(kernel, n_row, n_col), out_shape=jax.Sha...]
where the time goes in v4:
time: 38.8 us; the launch traced here: 38.6 us
  Pallas kernels  37 us (95%)
  other arithmetic  1.56 us (4%)
    pallas_call x1, Pallas kernels, shards(): pl.pallas_call(functools.partial(kernel, n_row, n_col), out_shape=jax.Sha...  37 us
    convert_element_type x1, other arithmetic, shards(): return mixed.astype(BF16)  1.56 us

profile of v4, /device:TPU:1, one launch (start us, length us, event | category | flops | bytes accessed | tf_op | source)
XLA Modules:
  0.0 38.6 jit_solution(1686761945990731866)
XLA Ops:
  0.0 37.0 %shard_map.154 = f32[4,40,192]{2,1,0:T(8,128)} custom-call(bf16[4,40,768]{2,1,0:T(8,128)(2,1)} %tokens_ref.1, bf16[40,384]{1,0:T(8,128)(2,1)} %single_ref.1, f32[2,384]{1,0:T(2,128)} %ada_gain_ref.1, f32[2,192]{1,0:T(2,128)} %scale_b_ref.1, f32[1,192]{1,0:T(1,128)} %bitcast.12, f32[2,192]{1,0:T(2,128)} %gate_b_ref.1, f32[1,128]{1,0:T(1,128)} %bitcast.13, ...), custom_call_target="tpu_custom_call" | custom-call | tf_op jit(solution)/shard_map/pallas_call | solution.py:497
  37.1 1.6 %convert_element_type.3 = bf16[4,40,192]{2,1,0:T(8,128)(2,1)} convert(f32[4,40,192]{2,1,0:T(8,128)} %shard_map.154) | non-fusion elementwise | flops 30720 | bytes 184320 | tf_op jit(solution)/shard_map/convert_element_type | solution.py:546
